TPU v7x, 512 devices: a whole 4x8x8 slice. The times are simulated.
512 devices in a mesh: row: 32 (over z, y_hi, core), col: 16 (over x, y_lo).
Axes of the slice: x: 4, y: 8 (y_hi: 2, y_lo: 4; y = y_hi * 4 + y_lo), z: 8, core: 2. Of those that a mesh axis runs over, the one named last changes fastest.
Arguments:
- query_state: float32 [65536, 256], P(('row', 'col')), may hold values from 0 to 2
- doc_state: float32 [16384, 256], P(('col', 'row')), may hold values from 0 to 2
- query_degree: int32 [65536], P(('row', 'col')), may hold values from 385 to 6144
- doc_degree: int32 [16384], P(('col', 'row')), may hold values from 1537 to 24576
- tile_slots: int32 [32, 16, 96], P('row', 'col'), may hold values from 0 to 127, as said below
- tile_count: int32 [32, 16], P('row', 'col'), may hold values from 16 to 96, as said below
- tile_bits: int32 [32, 16, 96, 128, 16], P('row', 'col'), may hold values from 0 to 255
- query_self_w: float32 [256, 256], replicated, may hold values from -0.375 to 0.375
- query_nbr_w: float32 [256, 256], replicated, may hold values from -0.375 to 0.375
- query_bias: float32 [256], replicated, may hold values from -0.5 to 0.5
- doc_self_w: float32 [256, 256], replicated, may hold values from -0.375 to 0.375
- doc_nbr_w: float32 [256, 256], replicated, may hold values from -0.375 to 0.375
- doc_bias: float32 [256], replicated, may hold values from -0.5 to 0.5
Outputs:
- query_out: float32 [65536, 256], P(('row', 'col'))
- doc_out: float32 [16384, 256], P(('col', 'row'))
Inputs may be any that keep to these rules, and one draw needn't show every extreme that they name: `tile_slots`: entries 0 to tile_count - 1 of a device's list are distinct and rising; slot s stands for its local query block s // 8 and local document block s % 8; the entries after them are other slots and stand for no tile. `tile_count`: some device holds 96 live tiles in every draw.
All inputs are finite; a program needn't handle non-finite values.
Results may differ from a plain program's by a relative error of at most 0.0003.
Values sent between devices are 32-bit elements; how exact they have to be, the bound alone decides.
A program may use at most 64 MiB of HBM per device.

v0:
```python
import math

import jax
import jax.numpy as jnp
from jax import lax
from jax.sharding import PartitionSpec as P

QT = 16
DT = 8
TMAX = 96


HIGHEST = lax.Precision.HIGHEST


def unpack(packed):
    columns = jnp.arange(128, dtype=jnp.int32)
    spread = jnp.repeat(packed, 8, axis=-1)
    return jnp.bitwise_and(jnp.right_shift(spread, columns % 8), 1).astype(jnp.float32)


def dense_layer(state_in, neighbours, self_weight, neighbour_weight, bias_row):
    before = jnp.dot(state_in, self_weight, precision=HIGHEST, preferred_element_type=jnp.float32)
    before = (
        before
        + jnp.dot(
            neighbours, neighbour_weight, precision=HIGHEST, preferred_element_type=jnp.float32
        )
        + bias_row
    )
    hidden = jnp.maximum(before, 0.0)
    return hidden * lax.rsqrt(jnp.mean(hidden * hidden, axis=-1, keepdims=True) + 1e-05)


def local(
    query_state,
    doc_state,
    query_degree,
    doc_degree,
    tile_slots,
    tile_count,
    tile_bits,
    query_self_w,
    query_nbr_w,
    query_bias,
    doc_self_w,
    doc_nbr_w,
    doc_bias,
):
    feature_count = query_state.shape[1]
    slot_ids = tile_slots[0, 0]
    live_count = tile_count[0, 0]
    live_slots = (jnp.arange(TMAX, dtype=jnp.int32) < live_count).astype(jnp.float32)
    tile_masks = unpack(tile_bits[0, 0]) * live_slots[:, None, None]
    query_local = slot_ids // DT
    doc_local = slot_ids % DT
    query_range = jnp.arange(QT, dtype=jnp.int32)
    doc_range = jnp.arange(DT, dtype=jnp.int32)
    group_size = math.gcd(TMAX, 16)
    group_total = (live_count + group_size - 1) // group_size
    doc_inverse = lax.rsqrt(doc_degree.astype(jnp.float32))[:, None]
    doc_cols = lax.all_gather(doc_state * doc_inverse, "row", axis=0, tiled=True).reshape(
        DT, 128, feature_count
    )

    def forward_group(group_no, running):
        begin_at = group_no * group_size
        tile_mask = lax.dynamic_slice_in_dim(tile_masks, begin_at, group_size, 0)
        query_ids = lax.dynamic_slice_in_dim(query_local, begin_at, group_size, 0)
        doc_ids = lax.dynamic_slice_in_dim(doc_local, begin_at, group_size, 0)
        product = jnp.einsum(
            "tqd,tdf->tqf", tile_mask, jnp.take(doc_cols, doc_ids, axis=0), precision=HIGHEST
        )
        one_hot = (query_ids[:, None] == query_range[None, :]).astype(jnp.float32)
        return running + jnp.einsum("tr,tqf->rqf", one_hot, product, precision=HIGHEST)

    partial_query = lax.fori_loop(
        0, group_total, forward_group, jnp.zeros((QT, 128, feature_count), jnp.float32)
    )
    partial_query = partial_query.reshape(QT * 128, feature_count)
    query_inverse = lax.rsqrt(query_degree.astype(jnp.float32))[:, None]
    summed = lax.psum_scatter(partial_query, "col", scatter_dimension=0, tiled=True)
    query_out = dense_layer(
        query_state, summed * query_inverse, query_self_w, query_nbr_w, query_bias
    )
    query_cols = lax.all_gather(query_out * query_inverse, "col", axis=0, tiled=True)
    query_tiles = query_cols.reshape(QT, 128, feature_count)

    def backward_group(group_no, running):
        begin_at = group_no * group_size
        tile_mask = lax.dynamic_slice_in_dim(tile_masks, begin_at, group_size, 0)
        query_ids = lax.dynamic_slice_in_dim(query_local, begin_at, group_size, 0)
        doc_ids = lax.dynamic_slice_in_dim(doc_local, begin_at, group_size, 0)
        product = jnp.einsum(
            "tqd,tqf->tdf", tile_mask, jnp.take(query_tiles, query_ids, axis=0), precision=HIGHEST
        )
        one_hot = (doc_ids[:, None] == doc_range[None, :]).astype(jnp.float32)
        return running + jnp.einsum("tc,tdf->cdf", one_hot, product, precision=HIGHEST)

    partial_doc = lax.fori_loop(
        0, group_total, backward_group, jnp.zeros((DT, 128, feature_count), jnp.float32)
    )
    doc_summed = lax.psum_scatter(
        partial_doc.reshape(DT * 128, feature_count), "row", scatter_dimension=0, tiled=True
    )
    doc_out = dense_layer(doc_state, doc_summed * doc_inverse, doc_self_w, doc_nbr_w, doc_bias)
    return (query_out, doc_out)


def solution(mesh):
    placed = (
        P(("row", "col"), None),
        P(("col", "row"), None),
        P(("row", "col")),
        P(("col", "row")),
        P("row", "col", None),
        P("row", "col"),
        P("row", "col", None, None, None),
        P(),
        P(),
        P(),
        P(),
        P(),
        P(),
    )
    return jax.shard_map(
        local,
        mesh=mesh,
        in_specs=placed,
        out_specs=(P(("row", "col"), None), P(("col", "row"), None)),
        check_vma=False,
    )
```

profile of v0, /device:TPU:6, one launch (start us, length us, event | category | flops | bytes accessed | tf_op | source)
XLA Modules:
  0.0 514.5 jit_solution(11701859568775223160)
XLA Ops:
  7.2 0.7 convert_rsqrt_fusion.1
  7.9 1.4 broadcast_multiply_fusion.3
  10.1 5.7 %fusion.36 = f32[96,128,128]{1,2,0:T(8,128)} fusion(f32[96]{0:T(128)S(1)} %compare_convert_fusion, s32[128]{0:T(128)S(1)} %and_select_fusion.1, s32[96,128,16]{1,2,0:T(8,128)} %bitcast.51), kind=kLoop, calls=%fused_computation.39 | loop fusion | flops 6291456 | bytes 7078784 | tf_op jit(solution)/shard_map/mul | solution.py:54
  15.9 6.6 %copy.17 = f32[96,128,128]{2,1,0:T(8,128)} copy(f32[96,128,128]{1,2,0:T(8,128)} %fusion.36) | data formatting | bytes 12582912
  22.5 79.8 %all-gather.3.cloned.1.call-done = f32[1024,256]{1,0:T(8,128)} async-done(((f32[32,256]{1,0:T(8,128)}), f32[1024,256]{1,0:T(8,128)}) %all-gather.3.cloned.1.call-update) | async-done | bytes 1048592 | tf_op jit(solution)/shard_map/all_gather | solution.py:62
  102.2 1.6 broadcast_in_dim.45
  103.9 28.2 %while.22 = (s32[]{:T(128)}, f32[16,128,256]{2,0,1:T(8,128)}, s32[]{:T(128)}, s32[96]{0:T(128)S(1)}, f32[96,128,128]{2,1,0:T(8,128)}, /*index=5*/s32[96]{0:T(128...) while((s32[]{:T(128)}, f32[16,128,256]{2,0,1:T(8,128)}, ...), condition=%wide.region_1.2_spmd.clone, body=%wide.region_0.1_spmd.clone.sunk | while | flops 907019648 | bytes 15733383 | solution.py:77
  104.7 3.3 fusion.69
  108.0 5.2 %fusion.70 = f32[16,128,256]{2,0,1:T(8,128)} fusion(f32[16,128,256]{2,0,1:T(8,128)} %get-tuple-element.286, f32[16,128,256]{2,1,0:T(8,128)S(1)} %fusion.69, s32[16]{0:T(128)S(1)} %dynamic_slice.37), kind=kOutput, calls=%fused_computation.8.clone.1 | convolution fusion | flops 101187840 | bytes 6291520 | tf_op jit(solution)/shard_map/while/body/tr,tqf->rqf/dot_general | solution.py:75
  114.0 3.3 fusion.69
  117.4 5.2 %fusion.70 = f32[16,128,256]{2,0,1:T(8,128)} fusion(f32[16,128,256]{2,0,1:T(8,128)} %get-tuple-element.286, f32[16,128,256]{2,1,0:T(8,128)S(1)} %fusion.69, s32[16]{0:T(128)S(1)} %dynamic_slice.37), kind=kOutput, calls=%fused_computation.8.clone.1 | convolution fusion | flops 101187840 | bytes 6291520 | tf_op jit(solution)/shard_map/while/body/tr,tqf->rqf/dot_general | solution.py:75
  123.4 3.3 fusion.69
  126.8 5.2 %fusion.70 = f32[16,128,256]{2,0,1:T(8,128)} fusion(f32[16,128,256]{2,0,1:T(8,128)} %get-tuple-element.286, f32[16,128,256]{2,1,0:T(8,128)S(1)} %fusion.69, s32[16]{0:T(128)S(1)} %dynamic_slice.37), kind=kOutput, calls=%fused_computation.8.clone.1 | convolution fusion | flops 101187840 | bytes 6291520 | tf_op jit(solution)/shard_map/while/body/tr,tqf->rqf/dot_general | solution.py:75
  132.0 4.2 copy.18
  137.5 108.5 %reduce-scatter.3.cloned.1.call-done = f32[128,256]{1,0:T(8,128)} async-done(((f32[2048,256]{1,0:T(8,128)}), f32[128,256]{1,0:T(8,128)}) %reduce-scatter.3.cloned.1.call-update) | async-done | bytes 131088 | tf_op jit(solution)/shard_map/reduce_scatter | solution.py:82
  246.1 1.3 multiply_reduce_fusion
  247.4 0.8 broadcast_multiply_fusion.1
  248.2 86.9 %all-gather.5.cloned.1.call-done = f32[2048,256]{1,0:T(8,128)} async-done(((f32[128,256]{1,0:T(8,128)}), f32[2048,256]{1,0:T(8,128)}) %all-gather.5.cloned.1.call-update) | async-done | bytes 2097168 | tf_op jit(solution)/shard_map/all_gather | solution.py:86
  335.2 24.8 %while.23 = (s32[]{:T(128)}, f32[8,128,256]{2,0,1:T(8,128)S(1)}, s32[]{:T(128)}, s32[96]{0:T(128)S(1)}, f32[96,128,128]{2,1,0:T(8,128)}, /*index=5*/s32[96]{0:T(...) while((s32[]{:T(128)}, f32[8,128,256]{2,0,1:T(8,128)S(1)}, ...), condition=%wide.region_5.6_spmd.clone, body=%wide.region_4.5_spmd.clone.sunk | while | flops 856425728 | bytes 13636231 | solution.py:100
  335.5 2.3 gather_fusion.1
  337.8 3.4 fusion.75
  341.3 2.3 fusion.76
  343.7 2.3 gather_fusion.1
  346.0 3.4 fusion.75
  349.5 2.3 fusion.76
  351.9 2.3 gather_fusion.1
  354.2 3.4 fusion.75
  357.7 2.3 fusion.76
  360.1 1.3 copy.20
  361.7 144.4 %reduce-scatter.5.cloned.1.call-done = f32[32,256]{1,0:T(8,128)} async-done(((f32[1024,256]{1,0:T(8,128)}), f32[32,256]{1,0:T(8,128)}) %reduce-scatter.5.cloned.1.call-update) | async-done | bytes 32784 | tf_op jit(solution)/shard_map/reduce_scatter | solution.py:103
  506.1 1.1 multiply_reduce_fusion.1
  507.3 0.7 broadcast_multiply_fusion.2
  (60 shorter events, 4.8 us)
Async XLA Ops:
  7.2 238.9 %copy-start = (f32[256,256]{1,0:T(8,128)S(1)}, f32[256,256]{1,0:T(8,128)}, u32[]{:S(2)}) copy-start(f32[256,256]{1,0:T(8,128)} %param.25) | copy-start | bytes 786436
  7.2 95.1 %all-gather.3.cloned.1.call-start = ((), (), s32[]{:S(2)}) async-start(), calls=%async_computation.2 | async-start | bytes 1081344 | tf_op jit(solution)/shard_map/all_gather | solution.py:62
  9.4 236.7 %reduce-scatter.3.cloned.1.call-start = ((), (), s32[]{:S(2)}) async-start(), calls=%async_computation.3 | async-start | bytes 2228224 | tf_op jit(solution)/shard_map/reduce_scatter | solution.py:82
  15.9 6.6 %copy-start.9 = (s32[1,1,96]{2,1,0:T(1,128)S(1)}, s32[1,1,96]{2,1,0:T(1,128)}, u32[]{:S(2)}) copy-start(s32[1,1,96]{2,1,0:T(1,128)} %param.21) | copy-start | bytes 1156
  102.2 1.6 copy-start.1
  136.2 0.7 copy-start.10
  136.2 1.0 copy-start.3
  136.2 1.0 copy-start.6
  136.2 109.8 %copy-start.7 = (f32[256]{0:T(256)S(1)}, f32[256]{0:T(256)}, u32[]{:S(2)}) copy-start(f32[256]{0:T(256)} %param.26) | copy-start | bytes 3076
  136.3 198.9 %all-gather.5.cloned.1.call-start = ((), (), s32[]{:S(2)}) async-start(), calls=%async_computation.4 | async-start | bytes 2228224 | tf_op jit(solution)/shard_map/all_gather | solution.py:86
  248.2 257.9 %reduce-scatter.5.cloned.1.call-start = ((), (), s32[]{:S(2)}) async-start(), calls=%async_computation.5 | async-start | bytes 1081344 | tf_op jit(solution)/shard_map/reduce_scatter | solution.py:103
  360.0 1.4 copy-start.2
  360.0 1.4 copy-start.5
  360.1 146.0 %copy-start.4 = (f32[256,256]{1,0:T(8,128)S(1)}, f32[256,256]{1,0:T(8,128)}, u32[]{:S(2)}) copy-start(f32[256,256]{1,0:T(8,128)} %param.28) | copy-start | bytes 786436
  360.1 146.0 %copy-start.8 = (f32[256]{0:T(256)S(1)}, f32[256]{0:T(256)}, u32[]{:S(2)}) copy-start(f32[256]{0:T(256)} %param.29) | copy-start | bytes 3076
Sparse Core Ops, SparseCore 0:
  12.0 90.2 all-gather.2
  136.4 109.6 reduce-scatter.2
  248.3 86.8 all-gather.4
  361.5 144.5 reduce-scatter.4
where the time goes:
time: 521 us; the launch traced here: 514 us
  waiting for transfers between devices  420 us (81%)
  matrix products  45.6 us (9%)
  local copies, waits for them, and re-layouts  24.1 us (5%)
  between operations  14.6 us (3%)
  other arithmetic  9.91 us (2%)
    reduce_scatter x1, waiting for transfers between devices, local(): lax.psum_scatter(partial_doc.reshape(DT * 128, feature_count), 'row', sca...  144 us
    reduce_scatter x1, waiting for transfers between devices, local(): lax.psum_scatter(partial_query, 'col', scatter_dimension=0, tiled=True)  109 us
    all_gather x1, waiting for transfers between devices, local(): lax.all_gather(query_out * query_inverse, 'col', axis=0, tiled=True)  86.9 us
    all_gather x1, waiting for transfers between devices, local(): lax.all_gather(doc_state * doc_inverse, 'row', axis=0, tiled=True)  79.8 us
    dot_general x3, matrix products, forward_group(): jnp.einsum('tr,tqf->rqf', one_hot, product, precision=HIGHEST)  15.7 us
  transfers between devices with their start and end apart: 4, of which 4 were waited for; matrix products, arithmetic and copies ran while one was open for 3% of the time, Pallas kernels for 0%

commit v1 on v0

v1 whole, which is shorter than its diff:
```python
import functools

import jax
import jax.numpy as jnp
from jax import lax
from jax.experimental import pallas as pl
from jax.experimental.pallas import tpu as pltpu
from jax.sharding import PartitionSpec as P

QT = 16
DT = 8
TMAX = 96
NX, NYL, NZ, NYH = 4, 4, 8, 2
MESH = pl.DeviceIdType.MESH
HIGHEST = lax.Precision.HIGHEST


def split_two(x):
    high = x.astype(jnp.bfloat16)
    low = (x - high.astype(jnp.float32)).astype(jnp.bfloat16)
    return high, low


def column_of(row_vector):
    n = row_vector.shape[1]
    i = lax.broadcasted_iota(jnp.int32, (n, n), 0)
    j = lax.broadcasted_iota(jnp.int32, (n, n), 1)
    return jnp.sum(jnp.where(i == j, row_vector, 0.0), axis=1, keepdims=True)


def rms(before):
    hidden = jnp.maximum(before, 0.0)
    return hidden * lax.rsqrt(jnp.mean(hidden * hidden, axis=-1, keepdims=True) + 1e-05)


def dot_full(a, b):
    return jnp.dot(a, b, precision=HIGHEST, preferred_element_type=jnp.float32)


def kernel(
    qs_ref, ds_ref, qdeg_ref, ddeg_ref, slots_ref, count_ref, bits_ref,
    qw_ref, qnw_ref, qb_ref, dw_ref, dnw_ref, db_ref,
    qo_ref, do_ref,
    at, dg, lhs, part, r2, rx, sx, ry, qg, wq, yd, rc, zd, rd, qself, dself,
    s1, v1, s1c, v1c, sx1, vx1, sx2, vx2, sy, vy, s3, v3, s4c, v4c, s4, v4,
):
    row = lax.axis_index("row")
    col = lax.axis_index("col")
    z0, h0, c0 = row // 4, (row // 2) % 2, row % 2
    x0, y0 = col // NYL, col % NYL
    m0 = z0 * 2 + h0
    sibling = (row + 1 - 2 * c0, col)

    def mate(k):
        dz, dh = k // 2, k % 2
        return (z0 + dz) % NZ * 2 + (h0 + dh) % 2

    def mate_from(k):
        dz, dh = k // 2, k % 2
        return (z0 + NZ - dz) % NZ * 2 + (h0 + dh) % 2

    def x_dev(dx):
        return (row, (x0 + dx + NX) % NX * NYL + y0)

    def y_dev(k):
        return (row, x0 * NYL + (y0 + k) % NYL)

    def send(src, dst, ssem, rsem, dev):
        copy = pltpu.make_async_remote_copy(
            src_ref=src, dst_ref=dst, send_sem=ssem, recv_sem=rsem, device_id=dev, device_id_type=MESH
        )
        copy.start()
        return copy

    def sent(src, dst, ssem, rsem):
        pltpu.make_async_remote_copy(
            src_ref=src, dst_ref=dst, send_sem=ssem, recv_sem=rsem, device_id=sibling, device_id_type=MESH
        ).wait_send()

    def got(src, dst, ssem, rsem):
        pltpu.make_async_remote_copy(
            src_ref=src, dst_ref=dst, send_sem=ssem, recv_sem=rsem, device_id=sibling, device_id_type=MESH
        ).wait_recv()

    barrier = pltpu.get_barrier_semaphore()

    def greet(dev):
        pl.semaphore_signal(barrier, inc=1, device_id=dev, device_id_type=MESH)

    greet(sibling)
    greet(x_dev(1))
    greet(x_dev(-1))
    for k in range(1, NYL):
        greet(y_dev(k))

    def greet_mate(k, _):
        greet((mate(k) * 2 + c0, col))
        return 0

    lax.fori_loop(1, NZ * NYH, greet_mate, 0)

    dinv = column_of(lax.rsqrt(ddeg_ref[...].astype(jnp.float32)))
    qinv_row = lax.rsqrt(qdeg_ref[...].astype(jnp.float32))
    qinv = column_of(qinv_row)
    scaled = ds_ref[...] * dinv
    for h in range(2):
        dg[h, row] = scaled[:, h * 128 : (h + 1) * 128]

    pl.semaphore_wait(barrier, 1 + 2 + NYL - 1 + NZ * NYH - 1)

    for h in range(2):
        send(dg.at[h, row], dg.at[h, row], s1c.at[h, 0], v1c.at[h, 0], sibling)

        def push(k, _, h=h):
            send(dg.at[h, row], dg.at[h, row], s1.at[h, k], v1.at[h, k], (mate(k) * 2 + c0, col))
            return 0

        lax.fori_loop(1, NZ * NYH, push, 0)

    shifts = lax.broadcasted_iota(jnp.int32, (8, 128), 0)
    count = count_ref[0, 0]

    def unpack(s, t):
        t_in = jnp.minimum(t, TMAX - 1)
        hit = jnp.logical_and(t < count, slots_ref[0, t_in] == s)
        keep = jnp.where(hit, 1, 0)
        words = bits_ref[t_in] * keep
        rows = []
        for w in range(16):
            spread = jnp.broadcast_to(words[w : w + 1, :], (8, 128))
            rows.append(jnp.bitwise_and(jnp.right_shift(spread, shifts), 1).astype(jnp.float32))
        tile = jnp.concatenate(rows, axis=0).astype(jnp.bfloat16)
        return tile, t + keep

    def unpack_pair(p, t):
        for half in range(2):
            for d in range(DT):
                tile, t = unpack((2 * p + half) * DT + d, t)
                at[p, d * 128 : (d + 1) * 128, half * 128 : (half + 1) * 128] = tile
        return t

    lax.fori_loop(0, QT // 2, unpack_pair, jnp.int32(0))

    qself[...] = dot_full(qs_ref[...], qw_ref[...]) + qb_ref[...]
    dself[...] = dot_full(ds_ref[...], dw_ref[...]) + db_ref[...]

    def forward_docs(h):
        def pass_on(k, _):
            r = mate_from(k) * 2 + c0
            got(dg.at[h, r], dg.at[h, r], s1.at[h, k], v1.at[h, k])
            send(dg.at[h, r], dg.at[h, r], s1c.at[h, k], v1c.at[h, k], sibling)
            return 0

        lax.fori_loop(1, NZ * NYH, pass_on, 0)

    def wait_docs(h):
        def one(k, _):
            r = mate_from(k) * 2 + 1 - c0
            got(dg.at[h, r], dg.at[h, r], s1c.at[h, k], v1c.at[h, k])
            return 0

        lax.fori_loop(0, NZ * NYH, one, 0)

    def multiply(h, x):
        for j in range(2):
            both = jnp.dot(lhs[...], at[2 * x + j], preferred_element_type=jnp.float32)
            whole = both[:128] + both[128:]
            part[h, 4 * x + 2 * j] = whole[:, :128]
            part[h, 4 * x + 2 * j + 1] = whole[:, 128:]

    xp, xm, xo = (x0 + 1) % NX, (x0 + NX - 1) % NX, (x0 + 2) % NX

    def start_x(h):
        docs = dg[h].reshape(DT * 128, 128).T
        high, low = split_two(docs)
        lhs[0:128, :] = high
        lhs[128:256, :] = low
        multiply(h, xo)
        send(part.at[h, pl.ds(4 * xo, 2)], r2.at[h, 0], sx1.at[h, 0], vx1.at[h, 0], x_dev(1))
        send(part.at[h, pl.ds(4 * xo + 2, 2)], r2.at[h, 1], sx1.at[h, 1], vx1.at[h, 1], x_dev(-1))
        multiply(h, xp)
        send(part.at[h, pl.ds(4 * xp + 2, 2)], rx.at[h, 0, 1], sx2.at[h, 0], vx2.at[h, 0], x_dev(1))
        multiply(h, xm)
        send(part.at[h, pl.ds(4 * xm, 2)], rx.at[h, 1, 0], sx2.at[h, 1], vx2.at[h, 1], x_dev(-1))
        multiply(h, x0)

    def second_x(h):
        got(r2.at[h, 0], r2.at[h, 0], sx1.at[h, 0], vx1.at[h, 0])
        part[h, pl.ds(4 * xp, 2)] += r2[h, 0]
        send(part.at[h, pl.ds(4 * xp, 2)], rx.at[h, 0, 0], sx2.at[h, 2], vx2.at[h, 2], x_dev(1))
        got(r2.at[h, 1], r2.at[h, 1], sx1.at[h, 1], vx1.at[h, 1])
        part[h, pl.ds(4 * xm + 2, 2)] += r2[h, 1]
        send(part.at[h, pl.ds(4 * xm + 2, 2)], rx.at[h, 1, 1], sx2.at[h, 3], vx2.at[h, 3], x_dev(-1))

    def start_y(h):
        for i, (a, b) in enumerate(((0, 1), (1, 0), (0, 0), (1, 1))):
            got(rx.at[h, a, b], rx.at[h, a, b], sx2.at[h, i], vx2.at[h, i])
        for b in range(2):
            sx[h, 2 * b : 2 * b + 2] = part[h, pl.ds(4 * x0 + 2 * b, 2)] + rx[h, 0, b] + rx[h, 1, b]
        for k in range(1, NYL):
            send(sx.at[h, (y0 + k) % NYL], ry.at[h, k - 1], sy.at[h, k - 1], vy.at[h, k - 1], y_dev(k))

    def end_y(h):
        for k in range(NYL - 1):
            got(ry.at[h, k], ry.at[h, k], sy.at[h, k], vy.at[h, k])
        return ((sx[h, y0] + ry[h, 0]) + (ry[h, 1] + ry[h, 2])) * qinv_row

    forward_docs(0)
    forward_docs(1)
    wait_docs(0)
    start_x(0)
    wait_docs(1)
    start_x(1)
    second_x(0)
    second_x(1)
    start_y(0)
    start_y(1)
    agg = jnp.concatenate([end_y(0).T, end_y(1).T], axis=1)

    query_out = rms(qself[...] + dot_full(agg, qnw_ref[...]))
    qo_ref[...] = query_out
    query_scaled = query_out * qinv
    for h in range(2):
        qg[h, col] = query_scaled[:, h * 128 : (h + 1) * 128]

    def share(h, block, sem, dev):
        send(qg.at[h, block], qg.at[h, block], s3.at[h, sem], v3.at[h, block], dev)

    def have(h, block):
        got(qg.at[h, block], qg.at[h, block], s3.at[h, 0], v3.at[h, block])

    def own_out(h):
        for k in range(1, NYL):
            share(h, col, k - 1, y_dev(k))
        share(h, col, 3, x_dev(1))
        share(h, col, 4, x_dev(-1))

    def y_on(h):
        for k in range(1, NYL):
            block = x0 * NYL + (y0 + NYL - k) % NYL
            have(h, block)
            share(h, block, 3 + 2 * k, x_dev(1))
            share(h, block, 4 + 2 * k, x_dev(-1))

    def x_on(h, k):
        y = (y0 + NYL - k) % NYL
        way = 1 - 2 * (y // 2)
        block = (x0 - way + NX) % NX * NYL + y
        have(h, block)
        share(h, block, 11 + k, x_dev(way))

    def x_rest(h):
        for k in range(NYL):
            y = (y0 + NYL - k) % NYL
            way = 1 - 2 * (y // 2)
            have(h, (x0 + way + NX) % NX * NYL + y)
        for y in range(NYL):
            have(h, xo * NYL + y)

    own_out(0)
    own_out(1)
    y_on(0)
    x_on(0, 0)
    y_on(1)
    for k in range(1, NYL):
        x_on(0, k)
    x_on(1, 0)
    x_rest(0)

    def back(h):
        for j in range(QT // 2):
            high, low = split_two(qg[h, 2 * j : 2 * j + 2].reshape(256, 128))
            wq[j, :, 0:128] = high
            wq[j, :, 128:256] = low

        def rows_of(i, _):
            total = jnp.zeros((256, 256), jnp.float32)
            for j in range(QT // 2):
                total += jnp.dot(at[j, pl.ds(i * 256, 256), :], wq[j], preferred_element_type=jnp.float32)
            whole = (total[:, :128] + total[:, 128:]).reshape(4, 2, 32, 128)
            yd[h, 0, pl.ds(i * 4, 4)] = whole[:, 0]
            yd[h, 1, pl.ds(i * 4, 4)] = whole[:, 1]
            return 0

        lax.fori_loop(0, 4, rows_of, 0)
        send(yd.at[h, 1 - c0], rc.at[h], s4c.at[h], v4c.at[h], sibling)

    def spread(h):
        got(rc.at[h], rc.at[h], s4c.at[h], v4c.at[h])
        zd[h] = yd[h, c0] + rc[h]

        def push(k, _):
            send(zd.at[h, mate(k)], rd.at[h, k], s4.at[h, k], v4.at[h, k], (mate(k) * 2 + c0, col))
            return 0

        lax.fori_loop(1, NZ * NYH, push, 0)

    def collect(h):
        def one(k, total):
            got(rd.at[h, k], rd.at[h, k], s4.at[h, k], v4.at[h, k])
            return total + rd[h, k]

        return lax.fori_loop(1, NZ * NYH, one, zd[h, m0])

    back(0)
    for k in range(1, NYL):
        x_on(1, k)
    spread(0)
    x_rest(1)
    back(1)
    spread(1)
    doc_agg = jnp.concatenate([collect(0), collect(1)], axis=1) * dinv
    do_ref[...] = rms(dself[...] + dot_full(doc_agg, dnw_ref[...]))

    for h in range(2):
        def out_docs(k, _, h=h):
            sent(dg.at[h, row], dg.at[h, row], s1.at[h, k], v1.at[h, k])
            sent(zd.at[h, 0], rd.at[h, k], s4.at[h, k], v4.at[h, k])
            return 0

        lax.fori_loop(1, NZ * NYH, out_docs, 0)

        def out_sibling(k, _, h=h):
            sent(dg.at[h, row], dg.at[h, row], s1c.at[h, k], v1c.at[h, k])
            return 0

        lax.fori_loop(0, NZ * NYH, out_sibling, 0)
        for i in range(2):
            sent(r2.at[h, i], r2.at[h, i], sx1.at[h, i], vx1.at[h, i])
        for i in range(4):
            sent(rx.at[h, 0, 0], rx.at[h, 0, 0], sx2.at[h, i], vx2.at[h, i])
        for k in range(NYL - 1):
            sent(ry.at[h, k], ry.at[h, k], sy.at[h, k], vy.at[h, k])

        def out_query(k, _, h=h):
            sent(qg.at[h, 0], qg.at[h, 0], s3.at[h, k], v3.at[h, 0])
            return 0

        lax.fori_loop(0, 15, out_query, 0)
        sent(rc.at[h], rc.at[h], s4c.at[h], v4c.at[h])


def local(
    query_state, doc_state, query_degree, doc_degree, tile_slots, tile_count, tile_bits,
    query_self_w, query_nbr_w, query_bias, doc_self_w, doc_nbr_w, doc_bias,
):
    f32, bf16 = jnp.float32, jnp.bfloat16
    vmem = pl.BlockSpec(memory_space=pltpu.VMEM)
    smem = pl.BlockSpec(memory_space=pltpu.SMEM)
    dma = pltpu.SemaphoreType.DMA
    bits = jnp.swapaxes(tile_bits[0, 0], 1, 2)
    return pl.pallas_call(
        kernel,
        out_shape=(
            jax.ShapeDtypeStruct((128, 256), f32),
            jax.ShapeDtypeStruct((32, 256), f32),
        ),
        in_specs=[vmem, vmem, vmem, vmem, smem, smem] + [vmem] * 7,
        out_specs=(vmem, vmem),
        scratch_shapes=[
            pltpu.VMEM((QT // 2, DT * 128, 256), bf16),
            pltpu.VMEM((2, 32, 32, 128), f32),
            pltpu.VMEM((256, DT * 128), bf16),
            pltpu.VMEM((2, QT, 128, 128), f32),
            pltpu.VMEM((2, 2, 2, 128, 128), f32),
            pltpu.VMEM((2, 2, 2, 2, 128, 128), f32),
            pltpu.VMEM((2, NYL, 128, 128), f32),
            pltpu.VMEM((2, NYL - 1, 128, 128), f32),
            pltpu.VMEM((2, QT, 128, 128), f32),
            pltpu.VMEM((QT // 2, 256, 256), bf16),
            pltpu.VMEM((2, 2, 16, 32, 128), f32),
            pltpu.VMEM((2, 16, 32, 128), f32),
            pltpu.VMEM((2, 16, 32, 128), f32),
            pltpu.VMEM((2, 16, 32, 128), f32),
            pltpu.VMEM((128, 256), f32),
            pltpu.VMEM((32, 256), f32),
            dma((2, 16)), dma((2, 16)), dma((2, 16)), dma((2, 16)),
            dma((2, 2)), dma((2, 2)), dma((2, 4)), dma((2, 4)),
            dma((2, 3)), dma((2, 3)), dma((2, 15)), dma((2, 16)),
            dma((2,)), dma((2,)), dma((2, 16)), dma((2, 16)),
        ],
        compiler_params=pltpu.CompilerParams(
            collective_id=0, has_side_effects=True, vmem_limit_bytes=40 << 20
        ),
    )(
        query_state, doc_state, query_degree.reshape(1, 128), doc_degree.reshape(1, 32),
        tile_slots[0], tile_count, bits,
        query_self_w, query_nbr_w, query_bias.reshape(1, 256),
        doc_self_w, doc_nbr_w, doc_bias.reshape(1, 256),
    )


def solution(mesh):
    placed = (
        P(("row", "col"), None),
        P(("col", "row"), None),
        P(("row", "col")),
        P(("col", "row")),
        P("row", "col", None),
        P("row", "col"),
        P("row", "col", None, None, None),
        P(),
        P(),
        P(),
        P(),
        P(),
        P(),
    )
    return jax.shard_map(
        local,
        mesh=mesh,
        in_specs=placed,
        out_specs=(P(("row", "col"), None), P(("col", "row"), None)),
        check_vma=False,
    )
```

time: 521 us -> 114 us (0.22)
  waiting for transfers between devices: 420 us -> 0 us
  Pallas kernels: 0 us -> 102 us
  matrix products: 45.6 us -> 0 us
  local copies, waits for them, and re-layouts: 24.1 us -> 8.55 us
  between operations: 14.6 us -> 1.34 us
  other arithmetic: 9.91 us -> 0 us
    reduce_scatter x2 -> x0, waiting for transfers between devices: 253 us -> none  [the longest x1 144 us: local(): lax.psum_scatter(partial_doc.reshape(DT * 128, feature_count), 'row', sca...]
    all_gather x2 -> x0, waiting for transfers between devices: 167 us -> none  [the longest x1 86.9 us: local(): lax.all_gather(query_out * query_inverse, 'col', axis=0, tiled=True)]
    pallas_call x0 -> x1, Pallas kernels: none -> 102 us  [local(): pl.pallas_call(kernel, out_shape=(jax.ShapeDtypeStruct((128, 256), f32),...]
    dot_general x16 -> x0, matrix products: 45.6 us -> none  [the longest x3 15.7 us: forward_group(): jnp.einsum('tr,tqf->rqf', one_hot, product, precision=HIGHEST)]
    gather x6 -> x0, local copies, waits for them, and re-layouts: 8.87 us -> none  [the longest x3 6.82 us: backward_group(): jnp.take(query_tiles, query_ids, axis=0)]
    mul x4 -> x0, other arithmetic: 8.67 us -> none  [the longest x1 5.73 us: local(): tile_masks = unpack(tile_bits[0, 0]) * live_slots[:, None, None]]
    while x2 -> x0, local copies, waits for them, and re-layouts: 5.5 us -> none  [the longest x1 4.19 us: local(): lax.fori_loop(0, group_total, forward_group, jnp.zeros((QT, 128, feature_...]
  transfers between devices with their start and end apart: 4 -> 0, of which waited for: 4 -> 0; matrix products, arithmetic and copies ran while one was open for 3% -> 0% of each run, Pallas kernels for 0% -> 0%
where the time goes in v1:
time: 114 us; the launch traced here: 112 us
  Pallas kernels  102 us (89%)
  local copies, waits for them, and re-layouts  8.55 us (8%)
  between operations  1.34 us (1%)
    pallas_call x1, Pallas kernels, local(): pl.pallas_call(kernel, out_shape=(jax.ShapeDtypeStruct((128, 256), f32),...  102 us
    unnamed x26, local copies, waits for them, and re-layouts  8.55 us

profile of v1, /device:TPU:6, one launch (start us, length us, event | category | flops | bytes accessed | tf_op | source)
XLA Modules:
  0.0 112.2 jit_solution(6919116343607854728)
XLA Ops:
  1.3 0.0 copy-start.8
  1.3 0.0 copy-start.10
  1.3 0.0 copy-start.11
  1.3 0.0 copy-start.7
  1.3 0.0 copy-start.9
  1.3 0.6 copy-done.8
  2.0 0.0 copy-done.10
  2.0 0.0 copy-done.11
  2.0 0.0 copy-done.7
  2.0 0.0 copy-done.9
  2.0 0.0 copy-start
  2.0 1.1 %copy-done = s32[1,1,96,128,16]{3,4,2,1,0:T(8,128)S(1)} copy-done((s32[1,1,96,128,16]{3,4,2,1,0:T(8,128)S(1)}, s32[1,1,96,128,16]{3,4,2,1,0:T(8,128)}, u32[]{:S(2)}) %copy-start) | copy-done | bytes 786456
  3.1 0.0 copy-start.1
  3.1 0.9 copy-done.1
  4.1 0.0 copy-start.2
  4.1 0.9 copy-done.2
  5.0 0.0 copy-start.3
  5.0 0.9 copy-done.3
  6.0 0.0 copy-start.4
  6.0 0.9 copy-done.4
  6.9 0.0 copy-start.5
  6.9 0.9 copy-done.5
  7.9 0.0 copy-start.6
  7.9 0.8 copy-done.6
  8.6 102.3 %shard_map.140 = (f32[128,256]{1,0:T(8,128)S(1)}, f32[32,256]{1,0:T(8,128)S(1)}) custom-call(f32[128,256]{1,0:T(8,128)S(1)} %copy-done.5, f32[32,256]{1,0:T(8,128)S(1)} %copy-done.6, s32[1,128]{1,0:T(1,128)S(1)} %bitcast.11, s32[1,32]{1,0:T(1,128)S(1)} %bitcast.12, s32[1,96]{1,0:T(1,128)S(1)} %bitcast.13, s32[1,1]{1,0:T(1,128)S(6)} %copy.17.count_ref, ...), custom_call_target="tpu_custom_call" | custom-call | tf_op jit(solution)/shard_map/pallas_call | solution.py:352
  110.9 0.7 copy.18
  111.6 0.6 copy.19
Async XLA Ops:
  1.3 0.7 copy-start.8
  1.3 0.7 copy-start.10
  1.3 0.7 copy-start.11
  1.3 0.7 copy-start.7
  1.3 0.7 copy-start.9
  2.0 1.1 %copy-start = (s32[1,1,96,128,16]{3,4,2,1,0:T(8,128)S(1)}, s32[1,1,96,128,16]{3,4,2,1,0:T(8,128)}, u32[]{:S(2)}) copy-start(s32[1,1,96,128,16]{3,4,2,1,0:T(8,128)} %param.19) | copy-start | bytes 2359300
  3.1 0.9 copy-start.1
  4.1 0.9 copy-start.2
  5.0 0.9 copy-start.3
  6.0 0.9 copy-start.4
  6.9 0.9 copy-start.5
  7.9 0.8 copy-start.6

commit v2 on v1

--- a/solution.py
+++ b/solution.py
@@ -206,9 +206,9 @@
         return ((sx[h, y0] + ry[h, 0]) + (ry[h, 1] + ry[h, 2])) * qinv_row
 
     forward_docs(0)
-    forward_docs(1)
     wait_docs(0)
     start_x(0)
+    forward_docs(1)
     wait_docs(1)
     start_x(1)
     second_x(0)
@@ -345,18 +345,27 @@
     query_self_w, query_nbr_w, query_bias, doc_self_w, doc_nbr_w, doc_bias,
 ):
     f32, bf16 = jnp.float32, jnp.bfloat16
-    vmem = pl.BlockSpec(memory_space=pltpu.VMEM)
     smem = pl.BlockSpec(memory_space=pltpu.SMEM)
     dma = pltpu.SemaphoreType.DMA
-    bits = jnp.swapaxes(tile_bits[0, 0], 1, 2)
+    args = (
+        query_state, doc_state, query_degree.reshape(1, 128), doc_degree.reshape(1, 32),
+        tile_slots[0], tile_count, jnp.swapaxes(tile_bits[0, 0], 1, 2),
+        query_self_w, query_nbr_w, query_bias.reshape(1, 256),
+        doc_self_w, doc_nbr_w, doc_bias.reshape(1, 256),
+    )
+
+    def whole(a):
+        return pl.BlockSpec(a.shape, lambda i: (0,) * len(a.shape))
+
     return pl.pallas_call(
         kernel,
         out_shape=(
             jax.ShapeDtypeStruct((128, 256), f32),
             jax.ShapeDtypeStruct((32, 256), f32),
         ),
-        in_specs=[vmem, vmem, vmem, vmem, smem, smem] + [vmem] * 7,
-        out_specs=(vmem, vmem),
+        grid=(1,),
+        in_specs=[smem if i in (4, 5) else whole(a) for i, a in enumerate(args)],
+        out_specs=(whole(query_state), whole(doc_state)),
         scratch_shapes=[
             pltpu.VMEM((QT // 2, DT * 128, 256), bf16),
             pltpu.VMEM((2, 32, 32, 128), f32),
@@ -380,14 +389,9 @@
             dma((2,)), dma((2,)), dma((2, 16)), dma((2, 16)),
         ],
         compiler_params=pltpu.CompilerParams(
-            collective_id=0, has_side_effects=True, vmem_limit_bytes=40 << 20
+            collective_id=0, has_side_effects=True, vmem_limit_bytes=56 << 20
         ),
-    )(
-        query_state, doc_state, query_degree.reshape(1, 128), doc_degree.reshape(1, 32),
-        tile_slots[0], tile_count, bits,
-        query_self_w, query_nbr_w, query_bias.reshape(1, 256),
-        doc_self_w, doc_nbr_w, doc_bias.reshape(1, 256),
-    )
+    )(*args)
 
 
 def solution(mesh):

time: 114 us -> 109 us (0.956)
  local copies, waits for them, and re-layouts: 8.55 us -> 2.19 us
  Pallas kernels: 102 us -> 104 us
    unnamed x26 -> x4, local copies, waits for them, and re-layouts: 8.55 us -> 2.19 us
    pallas_call x1, Pallas kernels: 102 us -> 104 us  [local(): pl.pallas_call(kernel, out_shape=(jax.ShapeDtypeStruct((128, 256), f32),...]
where the time goes in v2:
time: 109 us; the launch traced here: 108 us
  Pallas kernels  104 us (95%)
  local copies, waits for them, and re-layouts  2.19 us (2%)
  between operations  1.3 us (1%)
    pallas_call x1, Pallas kernels, local(): pl.pallas_call(kernel, out_shape=(jax.ShapeDtypeStruct((128, 256), f32),...  104 us
    unnamed x4, local copies, waits for them, and re-layouts  2.19 us

profile of v2, /device:TPU:6, one launch (start us, length us, event | category | flops | bytes accessed | tf_op | source)
XLA Modules:
  0.0 107.7 jit_solution(5999788391386604762)
XLA Ops:
  1.3 104.2 %shard_map.140 = (f32[128,256]{1,0:T(8,128)}, f32[32,256]{1,0:T(8,128)}) custom-call(f32[128,256]{1,0:T(8,128)} %qs_ref.1, f32[32,256]{1,0:T(8,128)} %ds_ref.1, s32[1,128]{1,0:T(1,128)} %bitcast.11, s32[1,32]{1,0:T(1,128)} %bitcast.12, s32[1,96]{1,0:T(1,128)} %bitcast.13, s32[1,1]{1,0:T(1,128)S(6)} %copy.17.count_ref, s32[96,16,128]{2,1,0:T(8,128)} %bitcast.8, ...), custom_call_target="tpu_custom_call" | custom-call | tf_op jit(solution)/shard_map/pallas_call | solution.py:360
  105.5 0.0 copy-start
  105.5 1.6 %copy.18 = f32[128,256]{1,0:T(8,128)} copy(f32[128,256]{1,0:T(8,128)} %get-tuple-element.4) | data formatting | bytes 262144
  107.1 0.0 copy-done
  107.1 0.6 copy.19
Async XLA Ops:
  105.5 1.6 %copy-start = (f32[32,256]{1,0:T(8,128)S(1)}, f32[32,256]{1,0:T(8,128)}, u32[]{:S(2)}) copy-start(f32[32,256]{1,0:T(8,128)} %get-tuple-element.5) | copy-start | bytes 98308

commit v3 on v2

--- a/solution.py
+++ b/solution.py
@@ -11,6 +11,7 @@
 DT = 8
 TMAX = 96
 NX, NYL, NZ, NYH = 4, 4, 8, 2
+Y_ORDER = (3, 2, 1)
 MESH = pl.DeviceIdType.MESH
 HIGHEST = lax.Precision.HIGHEST
 
@@ -197,7 +198,7 @@
             got(rx.at[h, a, b], rx.at[h, a, b], sx2.at[h, i], vx2.at[h, i])
         for b in range(2):
             sx[h, 2 * b : 2 * b + 2] = part[h, pl.ds(4 * x0 + 2 * b, 2)] + rx[h, 0, b] + rx[h, 1, b]
-        for k in range(1, NYL):
+        for k in Y_ORDER:
             send(sx.at[h, (y0 + k) % NYL], ry.at[h, k - 1], sy.at[h, k - 1], vy.at[h, k - 1], y_dev(k))
 
     def end_y(h):
@@ -230,13 +231,13 @@
         got(qg.at[h, block], qg.at[h, block], s3.at[h, 0], v3.at[h, block])
 
     def own_out(h):
-        for k in range(1, NYL):
+        for k in Y_ORDER:
             share(h, col, k - 1, y_dev(k))
         share(h, col, 3, x_dev(1))
         share(h, col, 4, x_dev(-1))
 
     def y_on(h):
-        for k in range(1, NYL):
+        for k in Y_ORDER:
             block = x0 * NYL + (y0 + NYL - k) % NYL
             have(h, block)
             share(h, block, 3 + 2 * k, x_dev(1))
@@ -262,9 +263,11 @@
     y_on(0)
     x_on(0, 0)
     y_on(1)
-    for k in range(1, NYL):
+    for k in Y_ORDER:
         x_on(0, k)
     x_on(1, 0)
+    for k in Y_ORDER:
+        x_on(1, k)
     x_rest(0)
 
     def back(h):
@@ -303,8 +306,6 @@
         return lax.fori_loop(1, NZ * NYH, one, zd[h, m0])
 
     back(0)
-    for k in range(1, NYL):
-        x_on(1, k)
     spread(0)
     x_rest(1)
     back(1)

time: 109 us -> 110 us (level)
  no operation moved by 1% of the time
where the time goes in v3:
time: 110 us; the launch traced here: 108 us
  Pallas kernels  105 us (95%)
  local copies, waits for them, and re-layouts  2.19 us (2%)
  between operations  1.3 us (1%)
    pallas_call x1, Pallas kernels, local(): pl.pallas_call(kernel, out_shape=(jax.ShapeDtypeStruct((128, 256), f32),...  105 us

profile of v3, /device:TPU:6, one launch (start us, length us, event | category | flops | bytes accessed | tf_op | source)
XLA Modules:
  0.0 108.4 jit_solution(7911198929022039103)
XLA Ops:
  1.3 104.9 %shard_map.140 = (f32[128,256]{1,0:T(8,128)}, f32[32,256]{1,0:T(8,128)}) custom-call(f32[128,256]{1,0:T(8,128)} %qs_ref.1, f32[32,256]{1,0:T(8,128)} %ds_ref.1, s32[1,128]{1,0:T(1,128)} %bitcast.11, s32[1,32]{1,0:T(1,128)} %bitcast.12, s32[1,96]{1,0:T(1,128)} %bitcast.13, s32[1,1]{1,0:T(1,128)S(6)} %copy.17.count_ref, s32[96,16,128]{2,1,0:T(8,128)} %bitcast.8, ...), custom_call_target="tpu_custom_call" | custom-call | tf_op jit(solution)/shard_map/pallas_call | solution.py:361
  106.2 0.0 copy-start
  106.2 1.6 %copy.18 = f32[128,256]{1,0:T(8,128)} copy(f32[128,256]{1,0:T(8,128)} %get-tuple-element.4) | data formatting | bytes 262144
  107.8 0.0 copy-done
  107.8 0.6 copy.19
Async XLA Ops:
  106.2 1.6 %copy-start = (f32[32,256]{1,0:T(8,128)S(1)}, f32[32,256]{1,0:T(8,128)}, u32[]{:S(2)}) copy-start(f32[32,256]{1,0:T(8,128)} %get-tuple-element.5) | copy-start | bytes 98308
